TPU v7x, 256 devices: a whole 4x4x8 slice. The times are simulated.
256 devices in a mesh: island: 16 (over y_hi, x, core), fsdp: 16 (over y_lo, z).
Axes of the slice: x: 4, y: 4 (y_hi: 2, y_lo: 2; y = y_hi * 2 + y_lo), z: 8, core: 2. Of those that a mesh axis runs over, the one named last changes fastest.
Arguments:
- normed: bfloat16 [2, 49152, 8192], P(None, ('island', 'fsdp')), may hold values from -6 to 6
- value_weight: bfloat16 [16, 8192, 512], P('island', 'fsdp'), may hold values from -0.0625 to 0.0625
- value_cotangent: bfloat16 [2, 49152, 512], P(None, ('island', 'fsdp')), may hold values from -0.079589844 to 0.079589844
- local_fragment: bfloat16 [16, 8192, 512], P('island', 'fsdp'), may hold values from -6 to 6
- global_fragment: float32 [8192, 512], P('fsdp'), may hold values from -6 to 6
- outer_momentum: float32 [8192, 512], P('fsdp', 'island'), may hold values from -3 to 3
Outputs:
- projected: bfloat16 [2, 49152, 512], P(None, ('island', 'fsdp'))
- value_grad: float32 [16, 8192, 512], P('island', 'fsdp')
- new_global: float32 [8192, 512], P('fsdp')
- new_momentum: float32 [8192, 512], P('fsdp', 'island')
All inputs are finite; a program needn't handle non-finite values.
Results may differ from a plain program's by a relative error of at most 0.001.
Values may be sent and summed in bfloat16 or wider, within the bound.
No kernel may reach another device: no remote copies, remote signals or barrier semaphores. Data moves between devices by JAX's collectives and lax.ppermute only.
A program may use at most 128 MiB of HBM per device.

v0:
```python
import jax
import jax.numpy as jnp
from jax import lax
from jax.sharding import PartitionSpec as P

outer_rate = 0.7
outer_mu = 0.9


def per_device(
    normed, value_weight, value_cotangent, local_fragment, global_fragment, outer_momentum
):
    micro_count, tok_rows, model_width = normed.shape
    kv_width = value_cotangent.shape[2]
    flat_rows = normed.reshape(micro_count * tok_rows, model_width)
    flat_cots = value_cotangent.reshape(micro_count * tok_rows, kv_width)
    columns = flat_rows
    forward = jnp.dot(
        columns,
        lax.all_gather(value_weight[0], "fsdp", axis=0, tiled=True),
        preferred_element_type=jnp.float32,
    )
    projected = forward.astype(jnp.bfloat16).reshape(micro_count, tok_rows, kv_width)
    columns = flat_rows
    gradient = lax.psum_scatter(
        lax.dot_general(
            columns, flat_cots, (((0,), (0,)), ((), ())), preferred_element_type=jnp.float32
        ),
        "fsdp",
        scatter_dimension=0,
        tiled=True,
    )
    value_grad = gradient[None]
    islands = lax.axis_size("island")
    own_delta = global_fragment - local_fragment[0].astype(jnp.float32)
    col_width = outer_momentum.shape[1]
    position = lax.axis_index("island")
    pseudo = lax.psum(own_delta, "island") / islands
    shared = lax.dynamic_slice_in_dim(pseudo, position * col_width, col_width, 1)
    new_momentum = outer_mu * outer_momentum + shared
    full_momentum = lax.all_gather(new_momentum, "island", axis=1, tiled=True)
    new_global = global_fragment - outer_rate * (pseudo + outer_mu * full_momentum)
    return (projected, value_grad, new_global, new_momentum)


def solution(mesh):
    placed = (
        P(None, ("island", "fsdp"), None),
        P("island", "fsdp", None),
        P(None, ("island", "fsdp"), None),
        P("island", "fsdp", None),
        P("fsdp", None),
        P("fsdp", "island"),
    )
    return jax.shard_map(
        per_device,
        mesh=mesh,
        in_specs=placed,
        out_specs=(
            P(None, ("island", "fsdp"), None),
            P("island", "fsdp", None),
            P("fsdp", None),
            P("fsdp", "island"),
        ),
        check_vma=False,
    )
```

profile of v0, /device:TPU:1, one launch (start us, length us, event | category | flops | bytes accessed | tf_op | source)
XLA Modules:
  0.0 510.5 jit_solution(15630123859144068690)
XLA Ops:
  7.2 0.0 copy-start
  7.2 0.0 copy-start.2
  7.2 0.0 all-reduce.2.cloned.1.call-start
  7.2 1.6 copy.12
  8.8 1.3 copy.10
  10.1 1.1 convert_subtract_fusion
  11.2 0.0 all-reduce.2.cloned.1.call-update
  11.3 0.0 all-gather.4.cloned.1.call-start
  11.3 149.2 %all-reduce.2.cloned.1.call-done = f32[512,512]{0,1:T(8,128)} async-done(((f32[512,512]{0,1:T(8,128)}), f32[512,512]{0,1:T(8,128)}) %all-reduce.2.cloned.1.call-update) | async-done | bytes 1048592 | tf_op jit(solution)/shard_map/psum | solution.py:38
  160.5 1.3 broadcast_multiply_fusion
  161.8 0.0 copy-done.2
  161.8 0.6 dynamic-slice_add_fusion
  162.5 0.0 all-gather.4.cloned.1.call-update
  162.5 0.0 all-gather.6.cloned.1.call-start
  162.6 0.7 all-gather.6.cloned.1.call-update
  163.2 0.0 reduce-scatter.2.cloned.1.call-start
  163.3 0.0 copy-done
  163.3 11.1 %convolution_bitcast_fusion = f32[8192,512]{1,0:T(8,128)} fusion(bf16[2,192,8192]{2,1,0:T(8,128)(2,1)} %param.6, bf16[2,192,512]{2,1,0:T(8,128)(2,1)S(1)} %copy-done), kind=kOutput, calls=%fused_computation | convolution fusion | flops 3221225472 | bytes 23461888 | tf_op jit(solution)/shard_map/dot_general | solution.py:26
  174.4 0.0 copy-start.1
  174.4 0.0 reduce-scatter.2.cloned.1.call-update
  174.4 41.6 %all-gather.4.cloned.1.call-done = f32[512,512]{0,1:T(8,128)} async-done(((f32[512,32]{0,1:T(8,128)}), f32[512,512]{0,1:T(8,128)}) %all-gather.4.cloned.1.call-update) | async-done | bytes 1048592 | tf_op jit(solution)/shard_map/all_gather | solution.py:41
  216.0 0.0 copy-done.1
  216.0 1.6 multiply_subtract_fusion
  217.6 1.3 copy.13
  218.9 98.5 %all-gather.6.cloned.1.call-done = bf16[1,8192,512]{2,1,0:T(8,128)(2,1)} async-done(((bf16[1,512,512]{2,1,0:T(8,128)(2,1)}), bf16[1,8192,512]{2,1,0:T(8,128)(2,1)}) %all-gather.6.cloned.1.call-update) | async-done | bytes 8388624 | tf_op jit(solution)/shard_map/all_gather | solution.py:20
  317.4 9.3 %fusion.2 = bf16[384,512]{1,0:T(8,128)(2,1)} fusion(bf16[384,8192]{1,0:T(8,128)(2,1)} %bitcast.16, bf16[1,8192,512]{2,1,0:T(8,128)(2,1)} %all-gather.6.cloned.1.call-done), kind=kOutput, calls=%fused_computation.3 | convolution fusion | flops 3221422080 | bytes 15073280 | tf_op jit(solution)/shard_map/dot_general | solution.py:18
  326.7 177.3 %reduce-scatter.2.cloned.1.call-done = f32[512,512]{1,0:T(8,128)} async-done(((f32[8192,512]{1,0:T(8,128)}), f32[512,512]{1,0:T(8,128)}) %reduce-scatter.2.cloned.1.call-update) | async-done | bytes 1048592 | tf_op jit(solution)/shard_map/reduce_scatter | solution.py:25
Async XLA Ops:
  7.2 156.1 %copy-start = (bf16[2,192,512]{2,1,0:T(8,128)(2,1)S(1)}, bf16[2,192,512]{2,1,0:T(8,128)(2,1)}, u32[]{:S(2)}) copy-start(bf16[2,192,512]{2,1,0:T(8,128)(2,1)} %param.8) | copy-start | bytes 1179652
  7.2 154.7 %copy-start.2 = (f32[512,32]{0,1:T(8,128)S(1)}, f32[512,32]{0,1:T(8,128)}, u32[]{:S(2)}) copy-start(f32[512,32]{0,1:T(8,128)} %param.11) | copy-start | bytes 196612
  7.2 153.3 %all-reduce.2.cloned.1.call-start = ((), (), s32[]{:S(2)}) async-start(), calls=%async_computation.2 | async-start | bytes 2097152 | tf_op jit(solution)/shard_map/psum | solution.py:38
  11.3 204.7 %all-gather.4.cloned.1.call-start = ((), (), s32[]{:S(2)}) async-start(), calls=%async_computation.3 | async-start | bytes 1114112 | tf_op jit(solution)/shard_map/all_gather | solution.py:41
  162.5 154.9 %all-gather.6.cloned.1.call-start = ((), (), s32[]{:S(2)}) async-start(), calls=%async_computation.4 | async-start | bytes 8912896 | tf_op jit(solution)/shard_map/all_gather | solution.py:20
  163.2 340.7 %reduce-scatter.2.cloned.1.call-start = ((), (), s32[]{:S(2)}) async-start(), calls=%async_computation.1 | async-start | bytes 17825792 | tf_op jit(solution)/shard_map/reduce_scatter | solution.py:25
  174.4 41.6 %copy-start.1 = (f32[512,512]{0,1:T(8,128)S(1)}, f32[512,512]{0,1:T(8,128)}, u32[]{:S(2)}) copy-start(f32[512,512]{0,1:T(8,128)} %all-reduce.2.cloned.1.call-done) | copy-start | bytes 3145732
Sparse Core Ops, SparseCore 0:
  11.4 149.0 all-reduce.1
  164.2 51.7 all-gather.3
  217.9 99.4 all-gather.5
  320.5 183.4 reduce-scatter.1
where the time goes:
time: 511 us
  waiting for transfers between devices  467 us (91%)
  matrix products  20.4 us (4%)
  between operations  13.8 us (3%)
    reduce_scatter x1, waiting for transfers between devices, per_device(): lax.psum_scatter(lax.dot_general(columns, flat_cots, (((0,), (0,)), ((),...  177 us
    psum x1, waiting for transfers between devices, per_device(): pseudo = lax.psum(own_delta, 'island') / islands  149 us
    all_gather x1, waiting for transfers between devices, per_device(): lax.all_gather(value_weight[0], 'fsdp', axis=0, tiled=True)  98.5 us
    all_gather x1, waiting for transfers between devices, per_device(): full_momentum = lax.all_gather(new_momentum, 'island', axis=1, tiled=True)  41.6 us
    dot_general x1, matrix products, per_device(): lax.dot_general(columns, flat_cots, (((0,), (0,)), ((), ())), preferred_e...  11.1 us
  transfers between devices with their start and end apart: 4, of which 4 were waited for; matrix products, arithmetic and copies ran while one was open for 5% of the time, Pallas kernels for 0%

commit v1 on v0

--- a/solution.py
+++ b/solution.py
@@ -38,7 +38,8 @@
     pseudo = lax.psum(own_delta, "island") / islands
     shared = lax.dynamic_slice_in_dim(pseudo, position * col_width, col_width, 1)
     new_momentum = outer_mu * outer_momentum + shared
-    full_momentum = lax.all_gather(new_momentum, "island", axis=1, tiled=True)
+    sent = jnp.stack([new_momentum] * lax.axis_size("island"))
+    full_momentum = jnp.concatenate(lax.all_to_all(sent, "island", 0, 0), axis=1)
     new_global = global_fragment - outer_rate * (pseudo + outer_mu * full_momentum)
     return (projected, value_grad, new_global, new_momentum)
 

time: 511 us -> 342 us (0.67)
  waiting for transfers between devices: 467 us -> 143 us
  blocking collectives: 0 us -> 155 us
    reduce_scatter x1, waiting for transfers between devices: 177 us -> 0.01 us  [per_device(): lax.psum_scatter(lax.dot_general(columns, flat_cots, (((0,), (0,)), ((),...]
    all_to_all x0 -> x1, blocking collectives: none -> 155 us  [per_device(): lax.all_to_all(sent, 'island', 0, 0)]
    all_gather x1, waiting for transfers between devices: 98.5 us -> 0.01 us  [per_device(): lax.all_gather(value_weight[0], 'fsdp', axis=0, tiled=True)]
    all_gather x1 -> x0, waiting for transfers between devices: 41.6 us -> none  [per_device(): full_momentum = lax.all_gather(new_momentum, 'island', axis=1, tiled=True)]
    psum x1, waiting for transfers between devices: 149 us -> 143 us  [per_device(): pseudo = lax.psum(own_delta, 'island') / islands]
  transfers between devices with their start and end apart: 4 -> 3, of which waited for: 4 -> 1; matrix products, arithmetic and copies ran while one was open for 5% -> 7% of each run, Pallas kernels for 0% -> 0%
where the time goes in v1:
time: 342 us
  blocking collectives  155 us (45%)
  waiting for transfers between devices  143 us (42%)
  matrix products  20.4 us (6%)
  between operations  15.6 us (5%)
  local copies, waits for them, and re-layouts  4.3 us (1%)
    all_to_all x1, blocking collectives, per_device(): lax.all_to_all(sent, 'island', 0, 0)  155 us
    psum x1, waiting for transfers between devices, per_device(): pseudo = lax.psum(own_delta, 'island') / islands  143 us
    dot_general x1, matrix products, per_device(): lax.dot_general(columns, flat_cots, (((0,), (0,)), ((), ())), preferred_e...  11.1 us
    dot_general x1, matrix products, per_device(): jnp.dot(columns, lax.all_gather(value_weight[0], 'fsdp', axis=0, tiled=Tr...  9.35 us
  transfers between devices with their start and end apart: 3, of which 1 were waited for; matrix products, arithmetic and copies ran while one was open for 7% of the time, Pallas kernels for 0%

profile of v1, /device:TPU:1, one launch (start us, length us, event | category | flops | bytes accessed | tf_op | source)
XLA Modules:
  0.0 342.2 jit_solution(3667573410706770057)
XLA Ops:
  8.0 0.0 copy-start
  8.0 0.0 all-reduce.2.cloned.1.call-start
  8.1 1.6 copy.12
  9.7 1.3 copy.10
  10.9 1.1 convert_subtract_fusion
  12.1 0.0 all-reduce.2.cloned.1.call-update
  12.1 0.0 all-gather.3.cloned.1.call-start
  12.1 0.5 all-gather.3.cloned.1.call-update
  12.7 0.0 reduce-scatter.2.cloned.1.call-start
  12.7 0.0 copy-done
  12.7 11.1 %convolution_bitcast_fusion = f32[8192,512]{1,0:T(8,128)} fusion(bf16[2,192,8192]{2,1,0:T(8,128)(2,1)} %param.6, bf16[2,192,512]{2,1,0:T(8,128)(2,1)S(1)} %copy-done), kind=kOutput, calls=%fused_computation | convolution fusion | flops 3221225472 | bytes 23461888 | tf_op jit(solution)/shard_map/dot_general | solution.py:26
  23.8 0.0 copy-start.3
  23.8 0.0 reduce-scatter.2.cloned.1.call-update
  23.8 142.8 %all-reduce.2.cloned.1.call-done = f32[512,512]{0,1:T(8,128)} async-done(((f32[512,512]{0,1:T(8,128)}), f32[512,512]{0,1:T(8,128)}) %all-reduce.2.cloned.1.call-update) | async-done | bytes 1048592 | tf_op jit(solution)/shard_map/psum | solution.py:38
  166.6 0.0 copy-start.1
  166.6 1.4 broadcast_multiply_fusion.1
  168.0 0.0 copy-done.3
  168.1 0.0 copy-start.2
  168.1 0.1 stack.2
  168.2 155.4 %all_to_all.5 = f32[16,512,32]{1,2,0:T(8,128)S(1)} all-to-all(f32[16,512,32]{1,2,0:T(8,128)S(1)} %stack.2), channel_id=1, replica_groups=mesh['island'=16,'fsdp'=16] {'island'}, dimensions={0} | all-to-all | bytes 2097152 | tf_op jit(solution)/shard_map/all_to_all | solution.py:42
  323.6 0.1 broadcast_multiply_fusion
  323.7 0.0 copy-done.1
  323.7 0.4 fusion.6
  324.1 1.3 copy.13
  325.4 0.0 all-gather.3.cloned.1.call-done
  325.4 9.3 %fusion.2 = bf16[384,512]{1,0:T(8,128)(2,1)} fusion(bf16[384,8192]{1,0:T(8,128)(2,1)} %bitcast.24, bf16[1,8192,512]{2,1,0:T(8,128)(2,1)} %all-gather.3.cloned.1.call-done), kind=kOutput, calls=%fused_computation.3 | convolution fusion | flops 3221422080 | bytes 15073280 | tf_op jit(solution)/shard_map/dot_general | solution.py:18
  334.8 0.0 copy-done.2
  334.8 0.0 reduce-scatter.2.cloned.1.call-done
  (1 shorter events, 0.0 us)
Async XLA Ops:
  8.0 4.7 %copy-start = (bf16[2,192,512]{2,1,0:T(8,128)(2,1)S(1)}, bf16[2,192,512]{2,1,0:T(8,128)(2,1)}, u32[]{:S(2)}) copy-start(bf16[2,192,512]{2,1,0:T(8,128)(2,1)} %param.8) | copy-start | bytes 1179652
  8.0 158.6 %all-reduce.2.cloned.1.call-start = ((), (), s32[]{:S(2)}) async-start(), calls=%async_computation.3 | async-start | bytes 2097152 | tf_op jit(solution)/shard_map/psum | solution.py:38
  12.1 313.3 %all-gather.3.cloned.1.call-start = ((), (), s32[]{:S(2)}) async-start(), calls=%async_computation.4 | async-start | bytes 8912896 | tf_op jit(solution)/shard_map/all_gather | solution.py:20
  12.7 322.1 %reduce-scatter.2.cloned.1.call-start = ((), (), s32[]{:S(2)}) async-start(), calls=%async_computation.2 | async-start | bytes 17825792 | tf_op jit(solution)/shard_map/reduce_scatter | solution.py:25
  23.8 144.2 %copy-start.3 = (f32[512,32]{0,1:T(8,128)S(1)}, f32[512,32]{0,1:T(8,128)}, u32[]{:S(2)}) copy-start(f32[512,32]{0,1:T(8,128)} %param.11) | copy-start | bytes 196612
  166.6 157.1 %copy-start.1 = (f32[512,512]{0,1:T(8,128)S(1)}, f32[512,512]{0,1:T(8,128)}, u32[]{:S(2)}) copy-start(f32[512,512]{0,1:T(8,128)} %all-reduce.2.cloned.1.call-done) | copy-start | bytes 3145732
  168.1 166.7 %copy-start.2 = (f32[512,32]{0,1:T(8,128)}, f32[512,32]{0,1:T(8,128)S(1)}, u32[]{:S(2)}) copy-start(f32[512,32]{0,1:T(8,128)S(1)} %dynamic-slice_add_fusion) | copy-start | bytes 196612
Sparse Core Ops, SparseCore 0:
  12.2 154.3 all-reduce.1
Sparse Core Ops, SparseCore 1:
  14.3 110.8 all-gather.2
  128.2 192.2 reduce-scatter.1

commit v2 on v0

--- a/solution.py
+++ b/solution.py
@@ -1,3 +1,4 @@
+import functools
 import jax
 import jax.numpy as jnp
 from jax import lax
@@ -5,6 +6,15 @@
 
 outer_rate = 0.7
 outer_mu = 0.9
+
+
+def mark_target(inner_x, peer_axis):
+    x_next = lax.all_gather(inner_x, axis_name=peer_axis)
+    p_next = jnp.sum(x_next, 0)
+    return p_next
+
+
+compute_paths = functools.partial(mark_target, peer_axis="island")
 
 
 def per_device(
@@ -35,7 +45,7 @@
     own_delta = global_fragment - local_fragment[0].astype(jnp.float32)
     col_width = outer_momentum.shape[1]
     position = lax.axis_index("island")
-    pseudo = lax.psum(own_delta, "island") / islands
+    pseudo = compute_paths(own_delta) / islands
     shared = lax.dynamic_slice_in_dim(pseudo, position * col_width, col_width, 1)
     new_momentum = outer_mu * outer_momentum + shared
     full_momentum = lax.all_gather(new_momentum, "island", axis=1, tiled=True)

time: 511 us -> 477 us (0.933)
  waiting for transfers between devices: 467 us -> 426 us
  other arithmetic: 4.69 us -> 12 us
    psum x1 -> x0, waiting for transfers between devices: 149 us -> none  [per_device(): pseudo = lax.psum(own_delta, 'island') / islands]
    all_gather x0 -> x1, waiting for transfers between devices: none -> 119 us  [mark_target(): x_next = lax.all_gather(inner_x, axis_name=peer_axis)]
    all_gather x1, waiting for transfers between devices: 98.5 us -> 79.8 us  [per_device(): lax.all_gather(value_weight[0], 'fsdp', axis=0, tiled=True)]
    reduce_sum x0 -> x1, other arithmetic: none -> 7.91 us  [mark_target(): p_next = jnp.sum(x_next, 0)]
    reduce_scatter x1, waiting for transfers between devices: 177 us -> 184 us  [per_device(): lax.psum_scatter(lax.dot_general(columns, flat_cots, (((0,), (0,)), ((),...]
  transfers between devices with their start and end apart: 4 -> 4, of which waited for: 4 -> 4; matrix products, arithmetic and copies ran while one was open for 5% -> 7% of each run, Pallas kernels for 0% -> 0%
where the time goes in v2:
time: 477 us; the launch traced here: 476 us
  waiting for transfers between devices  426 us (89%)
  matrix products  20.8 us (4%)
  between operations  13.8 us (3%)
  other arithmetic  12 us (3%)
    reduce_scatter x1, waiting for transfers between devices, per_device(): lax.psum_scatter(lax.dot_general(columns, flat_cots, (((0,), (0,)), ((),...  184 us
    all_gather x1, waiting for transfers between devices, mark_target(): x_next = lax.all_gather(inner_x, axis_name=peer_axis)  119 us
    all_gather x1, waiting for transfers between devices, per_device(): lax.all_gather(value_weight[0], 'fsdp', axis=0, tiled=True)  79.8 us
    all_gather x1, waiting for transfers between devices, per_device(): full_momentum = lax.all_gather(new_momentum, 'island', axis=1, tiled=True)  42.1 us
    dot_general x1, matrix products, per_device(): lax.dot_general(columns, flat_cots, (((0,), (0,)), ((), ())), preferred_e...  11.4 us
  transfers between devices with their start and end apart: 4, of which 4 were waited for; matrix products, arithmetic and copies ran while one was open for 7% of the time, Pallas kernels for 0%

profile of v2, /device:TPU:1, one launch (start us, length us, event | category | flops | bytes accessed | tf_op | source)
XLA Modules:
  0.0 476.4 jit_solution(10941836951331127705)
XLA Ops:
  7.2 0.0 copy-start
  7.2 0.0 all-gather.10.cloned.1.call-start
  7.2 2.5 convert_subtract_fusion
  9.8 0.0 all-gather.10.cloned.1.call-update
  9.8 0.0 all-gather.8.cloned.1.call-start
  9.8 0.7 all-gather.8.cloned.1.call-update
  10.5 0.0 all-gather.6.cloned.1.call-start
  10.6 1.0 copy.14
  11.6 119.4 %all-gather.10.cloned.1.call-done = f32[8192,512]{1,0:T(8,128)} async-done(((f32[512,512]{1,0:T(8,128)}), f32[8192,512]{1,0:T(8,128)}) %all-gather.10.cloned.1.call-update) | async-done | bytes 16777232 | tf_op jit(solution)/shard_map/all_gather | solution.py:12
  130.9 7.9 %reduce_sum.9 = f32[512,512]{1,0:T(8,128)S(1)} reduce(f32[16,512,512]{2,1,0:T(8,128)} %bitcast.17, f32[]{:T(128)} %constant.3.clone.1), dimensions={0}, to_apply=%region_1.0 | reduce | flops 3932160 | bytes 17825796 | tf_op jit(solution)/shard_map/reduce_sum | solution.py:13
  138.9 0.1 broadcast_multiply_fusion
  139.0 0.1 dynamic-slice_add_fusion
  139.1 0.7 copy.15
  139.8 0.0 all-gather.6.cloned.1.call-update
  139.9 0.0 reduce-scatter.2.cloned.1.call-start
  139.9 0.0 copy-done
  139.9 11.4 %convolution_bitcast_fusion = f32[8192,512]{1,0:T(8,128)} fusion(bf16[2,192,8192]{2,1,0:T(8,128)(2,1)} %param.6, bf16[2,192,512]{2,1,0:T(8,128)(2,1)S(1)} %copy-done), kind=kOutput, calls=%fused_computation | convolution fusion | flops 3221225472 | bytes 23461888 | tf_op jit(solution)/shard_map/dot_general | solution.py:36
  151.3 0.0 reduce-scatter.2.cloned.1.call-update
  151.3 79.8 %all-gather.8.cloned.1.call-done = bf16[1,8192,512]{2,1,0:T(8,128)(2,1)} async-done(((bf16[1,512,512]{2,1,0:T(8,128)(2,1)}), bf16[1,8192,512]{2,1,0:T(8,128)(2,1)}) %all-gather.8.cloned.1.call-update) | async-done | bytes 8388624 | tf_op jit(solution)/shard_map/all_gather | solution.py:30
  231.1 0.0 copy-start.1
  231.2 9.4 %fusion.2 = bf16[384,512]{1,0:T(8,128)(2,1)} fusion(bf16[384,8192]{1,0:T(8,128)(2,1)} %bitcast.18, bf16[1,8192,512]{2,1,0:T(8,128)(2,1)} %all-gather.8.cloned.1.call-done), kind=kOutput, calls=%fused_computation.3 | convolution fusion | flops 3221422080 | bytes 15073280 | tf_op jit(solution)/shard_map/dot_general | solution.py:28
  240.6 42.1 %all-gather.6.cloned.1.call-done = f32[512,512]{0,1:T(8,128)} async-done(((f32[512,32]{0,1:T(8,128)}), f32[512,512]{0,1:T(8,128)}) %all-gather.6.cloned.1.call-update) | async-done | bytes 1048592 | tf_op jit(solution)/shard_map/all_gather | solution.py:51
  282.7 1.6 copy.16
  284.3 0.0 copy-done.1
  284.3 1.3 multiply_subtract_fusion
  285.6 184.3 %reduce-scatter.2.cloned.1.call-done = f32[512,512]{1,0:T(8,128)} async-done(((f32[8192,512]{1,0:T(8,128)}), f32[512,512]{1,0:T(8,128)}) %reduce-scatter.2.cloned.1.call-update) | async-done | bytes 1048592 | tf_op jit(solution)/shard_map/reduce_scatter | solution.py:35
Async XLA Ops:
  7.2 132.8 %copy-start = (bf16[2,192,512]{2,1,0:T(8,128)(2,1)S(1)}, bf16[2,192,512]{2,1,0:T(8,128)(2,1)}, u32[]{:S(2)}) copy-start(bf16[2,192,512]{2,1,0:T(8,128)(2,1)} %param.8) | copy-start | bytes 1179652
  7.2 123.8 %all-gather.10.cloned.1.call-start = ((), (), s32[]{:S(2)}) async-start(), calls=%async_computation.4 | async-start | bytes 17825792 | tf_op jit(solution)/shard_map/all_gather | solution.py:12
  9.8 221.4 %all-gather.8.cloned.1.call-start = ((), (), s32[]{:S(2)}) async-start(), calls=%async_computation.3 | async-start | bytes 8912896 | tf_op jit(solution)/shard_map/all_gather | solution.py:30
  10.5 272.2 %all-gather.6.cloned.1.call-start = ((), (), s32[]{:S(2)}) async-start(), calls=%async_computation.2 | async-start | bytes 1114112 | tf_op jit(solution)/shard_map/all_gather | solution.py:51
  139.9 330.0 %reduce-scatter.2.cloned.1.call-start = ((), (), s32[]{:S(2)}) async-start(), calls=%async_computation.1 | async-start | bytes 17825792 | tf_op jit(solution)/shard_map/reduce_scatter | solution.py:35
  231.1 53.1 %copy-start.1 = (f32[512,512]{1,0:T(8,128)S(1)}, f32[512,512]{1,0:T(8,128)}, u32[]{:S(2)}) copy-start(f32[512,512]{1,0:T(8,128)} %param.10) | copy-start | bytes 3145732
Sparse Core Ops, SparseCore 0:
  11.3 119.5 all-gather.9
  132.7 98.3 all-gather.7
  234.5 48.2 all-gather.5
  285.7 184.1 reduce-scatter.1
